TPU v7x, 32 devices: a whole 2x2x4 slice. The times are simulated.
32 devices in a mesh: blk: 16 (over z, x, core), rep: 2 (over y).
Axes of the slice: x: 2, y: 2, z: 4, core: 2. Of those that a mesh axis runs over, the one named last changes fastest.
Arguments:
- features: bfloat16 [4096, 128], P('blk'), may hold values from -6 to 6
- tile_values: bfloat16 [16, 16, 16, 128, 128], P('blk', 'rep'), may hold values from -0.09375 to 0.09375
- tile_target: int32 [16, 16, 16], P('blk', 'rep'), may hold values from 0 to 1
- tile_source: int32 [16, 16, 16], P('blk', 'rep'), may hold values from 0 to 1
- tile_count: int32 [16, 16], P('blk', 'rep'), may hold values from 0 to 16, as said below
- hub_list: int32 [16, 16, 16], P('blk'), may hold values from 0 to 255
- hub_count: int32 [16, 16], P('blk'), may hold values from 0 to 16, as said below
- hub_weight: bfloat16 [16, 16, 4096], P(None, None, 'blk'), may hold values from -0.375 to 0.375
- self_weight: bfloat16 [128, 256], P(None, 'rep'), may hold values from -0.5 to 0.5
- neighbor_weight: bfloat16 [128, 256], P(None, 'rep'), may hold values from -0.5 to 0.5
- bias: float32 [256], P('rep'), may hold values from -3 to 3
- cotangent: bfloat16 [4096, 256], P('blk', 'rep'), may hold values from -6 to 6
Outputs:
- output: bfloat16 [4096, 256], P('blk', 'rep')
- grad_input: bfloat16 [4096, 128], P('blk')
- grad_self: float32 [128, 256], P(None, 'rep')
- grad_neighbor: float32 [128, 256], P(None, 'rep')
- grad_bias: float32 [256], P('rep')
Inputs may be any that keep to these rules, and one draw needn't show every extreme that they name: Slots at or beyond tile_count of a pair of blocks carry values that no output reads. Offset 0 of every destination block has all 16 slots live; some destination blocks may have many slots live at every offset. Coordinates may repeat within a pair; their terms add. `hub_list`: entries may repeat within one list; slots at or beyond hub_count are unused. `hub_count`: every sending block s uses all 16 slots for the reading block (s + 1) mod 16.
All inputs are finite; a program needn't handle non-finite values.
Results may differ from a plain program's by a relative error of at most 0.0056.
Values may be sent and summed in bfloat16 or wider, within the bound.
A program may use at most 64 MiB of HBM per device.

v0:
```python
import math

import jax
import jax.numpy as jnp
from jax import lax
from jax.sharding import PartitionSpec as P


def from_behind(block, axis, distance):
    devices = range(lax.axis_size(axis))
    route = [((i - distance) % len(devices), i) for i in devices]
    return lax.ppermute(block, axis, route)


def stop_tiles(tile_args, stop_index):
    tile_values, tile_target, tile_source, tile_count = tile_args
    tile_block = lax.dynamic_index_in_dim(tile_values[0], stop_index, 0, keepdims=False)
    target_tiles = lax.dynamic_index_in_dim(tile_target[0], stop_index, 0, keepdims=False)
    source_tiles = lax.dynamic_index_in_dim(tile_source[0], stop_index, 0, keepdims=False)
    filled = lax.dynamic_index_in_dim(tile_count[0], stop_index, 0, keepdims=False)
    active = (jnp.arange(tile_block.shape[0]) < filled).astype(jnp.float32)
    return (tile_block, target_tiles, source_tiles, active)


def forward_tiles(feature_block, totals, stop_tuple):
    tile_block, target_tiles, source_tiles, active = stop_tuple
    tile_rows, tile_size, feature_width = totals.shape
    picked = jnp.take(
        feature_block.reshape(tile_rows, tile_size, feature_width), source_tiles, axis=0
    )
    products = jnp.einsum("jab,jbf->jaf", tile_block, picked, preferred_element_type=jnp.float32)
    placer = jax.nn.one_hot(target_tiles, tile_rows, dtype=jnp.float32) * active[:, None]
    return totals + jnp.einsum("jt,jaf->taf", placer, products, precision=lax.Precision.HIGHEST)


def backward_tiles(grad_tiles, totals, stop_tuple):
    tile_block, target_tiles, source_tiles, active = stop_tuple
    picked = jnp.take(grad_tiles, target_tiles, axis=0)
    products = jnp.einsum("jab,jaf->jbf", tile_block, picked, preferred_element_type=jnp.float32)
    placer = jax.nn.one_hot(source_tiles, totals.shape[0], dtype=jnp.float32) * active[:, None]
    return totals + jnp.einsum("jt,jbf->tbf", placer, products, precision=lax.Precision.HIGHEST)


def on_device(
    features,
    tile_values,
    tile_target,
    tile_source,
    tile_count,
    hub_list,
    hub_count,
    hub_weight,
    self_weight,
    neighbor_weight,
    bias,
    cotangent,
):
    blocks = lax.axis_size("blk")
    half_cycle = blocks // 2
    rep_index = lax.axis_index("rep")
    rows_dev, feature_width = features.shape
    tile_size = tile_values.shape[-1]
    tile_rows = rows_dev // tile_size
    half_slots = hub_list.shape[-1] // 2
    tile_args = (tile_values, tile_target, tile_source, tile_count)
    zero_totals = jnp.zeros((tile_rows, tile_size, feature_width), jnp.float32)
    far_block = from_behind(features, "blk", half_cycle)
    start_block = jnp.where(rep_index == 1, far_block, features)

    def forward_body(stop_index, carried):
        feature_block, totals = carried
        totals = forward_tiles(feature_block, totals, stop_tiles(tile_args, stop_index))
        return (from_behind(feature_block, "blk", 1), totals)

    last_block, totals = lax.fori_loop(0, half_cycle - 1, forward_body, (start_block, zero_totals))
    totals = forward_tiles(last_block, totals, stop_tiles(tile_args, half_cycle - 1))
    slot_start = rep_index * half_slots
    send_lists = lax.dynamic_slice_in_dim(hub_list[0], slot_start, half_slots, 1)
    send_active = (slot_start + jnp.arange(half_slots))[None, :] < hub_count[0][:, None]
    hub_half = lax.dynamic_slice_in_dim(hub_weight, slot_start, half_slots, 1)
    outgoing = jnp.take(features, send_lists.reshape(-1), axis=0).reshape(
        blocks, half_slots, feature_width
    )
    outgoing = jnp.where(send_active[:, :, None], outgoing, jnp.zeros_like(outgoing))
    incoming = lax.all_to_all(outgoing, "blk", split_axis=0, concat_axis=0, tiled=True)
    hub_term = jnp.einsum("sjn,sjf->nf", hub_half, incoming, preferred_element_type=jnp.float32)
    rep_partial = totals.reshape(rows_dev, feature_width) + hub_term
    aggregate = lax.psum(rep_partial, "rep").astype(jnp.bfloat16)
    pre_activation = (
        jnp.dot(features, self_weight, preferred_element_type=jnp.float32)
        + jnp.dot(aggregate, neighbor_weight, preferred_element_type=jnp.float32)
        + bias
    )
    output = jax.nn.silu(pre_activation).astype(jnp.bfloat16)
    gate_value = jax.nn.sigmoid(pre_activation)
    grad_activation = (
        cotangent.astype(jnp.float32) * gate_value * (1.0 + pre_activation * (1.0 - gate_value))
    ).astype(jnp.bfloat16)
    grad_scale = 1.0 / math.sqrt(rows_dev * blocks)
    weight_terms = lax.psum(
        (
            jnp.einsum("nf,nh->fh", features, grad_activation, preferred_element_type=jnp.float32),
            jnp.einsum("nf,nh->fh", aggregate, grad_activation, preferred_element_type=jnp.float32),
            jnp.sum(grad_activation.astype(jnp.float32), axis=0),
        ),
        "blk",
    )
    grad_part = jnp.einsum(
        "nh,fh->nf", grad_activation, neighbor_weight, preferred_element_type=jnp.float32
    )
    grad_aggregate = lax.psum(grad_part, "rep")
    self_grad = jnp.einsum(
        "nh,fh->nf", grad_activation, self_weight, preferred_element_type=jnp.float32
    )
    grad_aggregate = grad_aggregate.astype(jnp.bfloat16)
    grad_tiles = grad_aggregate.reshape(tile_rows, tile_size, feature_width)

    def backward_body(stop_index, totals):
        totals = backward_tiles(grad_tiles, totals, stop_tiles(tile_args, stop_index))
        return from_behind(totals, "blk", 1)

    totals = lax.fori_loop(0, half_cycle, backward_body, zero_totals)
    back_terms = jnp.einsum(
        "sjn,nf->sjf", hub_half, grad_aggregate, preferred_element_type=jnp.float32
    )
    returned = lax.all_to_all(back_terms, "blk", split_axis=0, concat_axis=0, tiled=True)
    returned = jnp.where(send_active[:, :, None], returned, jnp.zeros((), jnp.float32))
    hub_grad = jax.ops.segment_sum(
        returned.reshape(-1, feature_width), send_lists.reshape(-1), num_segments=rows_dev
    )
    shifted_back = from_behind(totals, "blk", half_cycle)
    rep_terms = jnp.where(rep_index == 0, shifted_back, totals).reshape(rows_dev, feature_width)
    rep_terms = rep_terms + hub_grad
    grad_input = lax.psum(rep_terms + self_grad, "rep")
    return (
        output,
        grad_input.astype(jnp.bfloat16),
        weight_terms[0] * grad_scale,
        weight_terms[1] * grad_scale,
        weight_terms[2] * grad_scale,
    )


def solution(mesh):
    in_specs = (
        P("blk", None),
        P("blk", "rep", None, None, None),
        P("blk", "rep", None),
        P("blk", "rep", None),
        P("blk", "rep"),
        P("blk", None, None),
        P("blk", None),
        P(None, None, "blk"),
        P(None, "rep"),
        P(None, "rep"),
        P("rep"),
        P("blk", "rep"),
    )
    out_specs = (P("blk", "rep"), P("blk", None), P(None, "rep"), P(None, "rep"), P("rep"))
    return jax.shard_map(
        on_device, mesh=mesh, in_specs=in_specs, out_specs=out_specs, check_vma=False
    )
```

profile of v0, /device:TPU:26, one launch (start us, length us, event | category | flops | bytes accessed | tf_op | source)
XLA Modules:
  0.0 351.8 jit_solution(388536092360890582)
XLA Ops:
  8.5 1.5 gather_fusion.2
  11.6 6.2 %all-to-all-start = ((bf16[16,8,128]{2,1,0:T(8,128)(2,1)}), bf16[16,8,128]{2,1,0:T(8,128)(2,1)S(1)}, u32[]{:S(2)}, u32[]{:S(2)}) async-start(bf16[16,8,128]{2,1,0:T(8,128)(2,1)} %fusion.49), calls=%async_computation | async-start | bytes 65536 | tf_op jit(solution)/shard_map/all_to_all | solution.py:85
  23.1 52.0 %while.30 = (s32[]{:T(128)}, bf16[256,128]{1,0:T(8,128)(2,1)S(1)}, f32[2,128,128]{2,0,1:T(2,128)S(1)}, s32[1,8,16]{2,1,0:T(8,128)}, s32[1,8]{1,0:T(1,128)}, /*in...) while((s32[]{:T(128)}, bf16[256,128]{1,0:T(8,128)(2,1)S(1)}, ...), condition=%wide.region_1.3_spmd.clone, body=%wide.region_0.2_spmd.clone.sunk | while | flops 73729216 | bytes 4855047 | solution.py:75
  44.3 1.7 collective-permute-start.1
  56.9 1.4 fusion.105
  59.8 1.5 collective-permute-start.1
  65.2 1.4 fusion.105
  75.8 1.7 convolution_bitcast_fusion
  79.0 9.5 %all-reduce.7 = bf16[256,128]{1,0:T(8,128)(2,1)S(1)} all-reduce(f32[256,128]{1,0:T(8,128)S(1)} %fusion.37), channel_id=1, replica_groups=mesh['blk'=16,'rep'=2] {'rep'}, use_global_device_ids=true, to_apply=%region_2.4 | all-reduce | flops 32768 | bytes 196608 | tf_op jit(solution)/shard_map/psum | solution.py:88
  91.1 9.5 %all-reduce.8 = bf16[256,128]{1,0:T(8,128)(2,1)S(1)} all-reduce(f32[256,128]{1,0:T(8,128)S(1)} %fusion.67), channel_id=1, replica_groups=mesh['blk'=16,'rep'=2] {'rep'}, use_global_device_ids=true, to_apply=%region_3.5 | all-reduce | flops 32768 | bytes 196608 | tf_op jit(solution)/shard_map/psum | solution.py:111
  101.5 95.9 %while.29 = (s32[]{:T(128)}, f32[2,128,128]{2,0,1:T(2,128)S(1)}, s32[1,8,16]{2,1,0:T(8,128)}, s32[1,8]{1,0:T(1,128)S(1)}, bf16[1,8,16,128,128]{4,3,2,1,0:T(8,128...) while((s32[]{:T(128)}, f32[2,128,128]{2,0,1:T(2,128)S(1)}, ...), condition=%wide.region_5.7_spmd, body=%wide.region_4.6_spmd.sunk | while | flops 73696448 | bytes 4986101 | solution.py:122
  105.0 1.4 fusion.99
  107.7 4.4 %collective-permute-done = f32[2,128,128]{2,0,1:T(2,128)S(1)} collective-permute-done((f32[2,128,128]{2,0,1:T(2,128)S(1)}, f32[2,128,128]{2,0,1:T(2,128)S(1)}, u32[]{:S(2)}, u32[]{:S(2)}) %collective-permute-start) | collective-permute-done | bytes 131104 | tf_op jit(solution)/shard_map/while/body/eval_jaxpr/ppermute | solution.py:12
  115.5 1.4 fusion.99
  118.2 4.4 %collective-permute-done = f32[2,128,128]{2,0,1:T(2,128)S(1)} collective-permute-done((f32[2,128,128]{2,0,1:T(2,128)S(1)}, f32[2,128,128]{2,0,1:T(2,128)S(1)}, u32[]{:S(2)}, u32[]{:S(2)}) %collective-permute-start) | collective-permute-done | bytes 131104 | tf_op jit(solution)/shard_map/while/body/eval_jaxpr/ppermute | solution.py:12
  126.0 1.4 fusion.99
  128.6 1.9 collective-permute-start
  130.5 2.6 collective-permute-done
  136.5 1.4 fusion.99
  139.1 4.6 %collective-permute-start = (f32[2,128,128]{2,0,1:T(2,128)S(1)}, f32[2,128,128]{2,0,1:T(2,128)S(1)}, u32[]{:S(2)}, u32[]{:S(2)}) collective-permute-start(f32[2,128,128]{2,0,1:T(2,128)S(1)} %convolution_add_fusion.5), channel_id=1, source_target_pairs={{30,0},{0,2},{2,4},{4,6},{6,8},{8,10},{10,12},{12,14},{14,16},{16,... | collective-permute-start | bytes 393224 | tf_op jit(solution)/shard_map/while/body/eval_jaxpr/ppermute | solution.py:12
  148.1 1.4 fusion.99
  150.7 6.2 %collective-permute-start = (f32[2,128,128]{2,0,1:T(2,128)S(1)}, f32[2,128,128]{2,0,1:T(2,128)S(1)}, u32[]{:S(2)}, u32[]{:S(2)}) collective-permute-start(f32[2,128,128]{2,0,1:T(2,128)S(1)} %convolution_add_fusion.5), channel_id=1, source_target_pairs={{30,0},{0,2},{2,4},{4,6},{6,8},{8,10},{10,12},{12,14},{14,16},{16,... | collective-permute-start | bytes 393224 | tf_op jit(solution)/shard_map/while/body/eval_jaxpr/ppermute | solution.py:12
  161.3 1.4 fusion.99
  163.9 6.2 %collective-permute-start = (f32[2,128,128]{2,0,1:T(2,128)S(1)}, f32[2,128,128]{2,0,1:T(2,128)S(1)}, u32[]{:S(2)}, u32[]{:S(2)}) collective-permute-start(f32[2,128,128]{2,0,1:T(2,128)S(1)} %convolution_add_fusion.5), channel_id=1, source_target_pairs={{30,0},{0,2},{2,4},{4,6},{6,8},{8,10},{10,12},{12,14},{14,16},{16,... | collective-permute-start | bytes 393224 | tf_op jit(solution)/shard_map/while/body/eval_jaxpr/ppermute | solution.py:12
  174.5 1.4 fusion.99
  177.1 6.2 %collective-permute-start = (f32[2,128,128]{2,0,1:T(2,128)S(1)}, f32[2,128,128]{2,0,1:T(2,128)S(1)}, u32[]{:S(2)}, u32[]{:S(2)}) collective-permute-start(f32[2,128,128]{2,0,1:T(2,128)S(1)} %convolution_add_fusion.5), channel_id=1, source_target_pairs={{30,0},{0,2},{2,4},{4,6},{6,8},{8,10},{10,12},{12,14},{14,16},{16,... | collective-permute-start | bytes 393224 | tf_op jit(solution)/shard_map/while/body/eval_jaxpr/ppermute | solution.py:12
  187.6 1.4 fusion.99
  190.3 6.2 %collective-permute-start = (f32[2,128,128]{2,0,1:T(2,128)S(1)}, f32[2,128,128]{2,0,1:T(2,128)S(1)}, u32[]{:S(2)}, u32[]{:S(2)}) collective-permute-start(f32[2,128,128]{2,0,1:T(2,128)S(1)} %convolution_add_fusion.5), channel_id=1, source_target_pairs={{30,0},{0,2},{2,4},{4,6},{6,8},{8,10},{10,12},{12,14},{14,16},{16,... | collective-permute-start | bytes 393224 | tf_op jit(solution)/shard_map/while/body/eval_jaxpr/ppermute | solution.py:12
  197.4 15.3 %all-to-all-start.1 = ((f32[16,8,128]{2,1,0:T(8,128)}), f32[16,8,128]{2,1,0:T(8,128)S(1)}, u32[]{:S(2)}, u32[]{:S(2)}) async-start(f32[16,8,128]{2,1,0:T(8,128)} %fusion.46), calls=%async_computation.1 | async-start | bytes 131072 | tf_op jit(solution)/shard_map/all_to_all | solution.py:126
  212.8 26.3 %psum.47 = f32[128]{0:T(128)S(1)} all-reduce(f32[128]{0:T(128)S(1)} %get-tuple-element.350), channel_id=1, replica_groups=mesh['blk'=16,'rep'=2] {'blk'}, use_global_device_ids=true, to_apply=%region_11.13 | all-reduce | flops 128 | bytes 1024 | tf_op jit(solution)/shard_map/psum | solution.py:100
  239.6 91.1 %all-reduce.6.cloned.1.call-done = (f32[128,128]{0,1:T(8,128)}, f32[128,128]{0,1:T(8,128)}) async-done(((f32[128,128]{0,1:T(8,128)}, f32[128,128]{0,1:T(8,128)}), (f32[128,128]{0,1:T(8,128)}, f32[128,128]{0,1:T(8,128)})) %all-reduce.6.cloned.1.call-update) | async-done | bytes 131088 | tf_op jit(solution)/shard_map/psum | solution.py:100
  334.8 10.2 %all-reduce.9 = bf16[256,128]{1,0:T(8,128)(2,1)} all-reduce(f32[256,128]{1,0:T(8,128)S(1)} %scatter_custom_fusion), channel_id=1, replica_groups=mesh['blk'=16,'rep'=2] {'rep'}, use_global_device_ids=true, to_apply=%region_7.9 | all-reduce | flops 32768 | bytes 196608 | tf_op jit(solution)/shard_map/psum | solution.py:134
  (198 shorter events, 105.5 us)
Async XLA Ops:
  7.2 10.8 %copy-start = (bf16[16,16,256]{2,1,0:T(8,128)(2,1)S(1)}, bf16[16,16,256]{2,1,0:T(8,128)(2,1)}, u32[]{:S(2)}) copy-start(bf16[16,16,256]{2,1,0:T(8,128)(2,1)} %param.25) | copy-start | bytes 393220
  7.2 15.1 %collective-permute-start.2 = (bf16[256,128]{1,0:T(8,128)(2,1)}, bf16[256,128]{1,0:T(8,128)(2,1)S(1)}, u32[]{:S(2)}, u32[]{:S(2)}) collective-permute-start(bf16[256,128]{1,0:T(8,128)(2,1)} %param.18), channel_id=1, source_target_pairs={{16,0},{18,2},{20,4},{22,6},{24,8},{26,10},{28,12},{30,14},{0,16},... | collective-permute-start | bytes 196616 | tf_op jit(solution)/shard_map/ppermute | solution.py:12
  11.6 67.2 %all-to-all-start = ((bf16[16,8,128]{2,1,0:T(8,128)(2,1)}), bf16[16,8,128]{2,1,0:T(8,128)(2,1)S(1)}, u32[]{:S(2)}, u32[]{:S(2)}) async-start(bf16[16,8,128]{2,1,0:T(8,128)(2,1)} %fusion.49), calls=%async_computation | async-start | bytes 65536 | tf_op jit(solution)/shard_map/all_to_all | solution.py:85
  23.1 7.0 %collective-permute-start.1 = (bf16[256,128]{1,0:T(8,128)(2,1)S(1)}, bf16[256,128]{1,0:T(8,128)(2,1)S(1)}, u32[]{:S(2)}, u32[]{:S(2)}) collective-permute-start(bf16[256,128]{1,0:T(8,128)(2,1)S(1)} %copy.94), channel_id=1, source_target_pairs={{30,0},{0,2},{2,4},{4,6},{6,8},{8,10},{10,12},{12,14},{14,16},{16,... | collective-permute-start | bytes 196616 | tf_op jit(solution)/shard_map/while/body/eval_jaxpr/ppermute | solution.py:12
  30.1 6.9 %collective-permute-start.1 = (bf16[256,128]{1,0:T(8,128)(2,1)S(1)}, bf16[256,128]{1,0:T(8,128)(2,1)S(1)}, u32[]{:S(2)}, u32[]{:S(2)}) collective-permute-start(bf16[256,128]{1,0:T(8,128)(2,1)S(1)} %copy.94), channel_id=1, source_target_pairs={{30,0},{0,2},{2,4},{4,6},{6,8},{8,10},{10,12},{12,14},{14,16},{16,... | collective-permute-start | bytes 196616 | tf_op jit(solution)/shard_map/while/body/eval_jaxpr/ppermute | solution.py:12
  37.0 7.2 %collective-permute-start.1 = (bf16[256,128]{1,0:T(8,128)(2,1)S(1)}, bf16[256,128]{1,0:T(8,128)(2,1)S(1)}, u32[]{:S(2)}, u32[]{:S(2)}) collective-permute-start(bf16[256,128]{1,0:T(8,128)(2,1)S(1)} %copy.94), channel_id=1, source_target_pairs={{30,0},{0,2},{2,4},{4,6},{6,8},{8,10},{10,12},{12,14},{14,16},{16,... | collective-permute-start | bytes 196616 | tf_op jit(solution)/shard_map/while/body/eval_jaxpr/ppermute | solution.py:12
  44.3 8.5 %collective-permute-start.1 = (bf16[256,128]{1,0:T(8,128)(2,1)S(1)}, bf16[256,128]{1,0:T(8,128)(2,1)S(1)}, u32[]{:S(2)}, u32[]{:S(2)}) collective-permute-start(bf16[256,128]{1,0:T(8,128)(2,1)S(1)} %copy.94), channel_id=1, source_target_pairs={{30,0},{0,2},{2,4},{4,6},{6,8},{8,10},{10,12},{12,14},{14,16},{16,... | collective-permute-start | bytes 196616 | tf_op jit(solution)/shard_map/while/body/eval_jaxpr/ppermute | solution.py:12
  52.8 7.0 %collective-permute-start.1 = (bf16[256,128]{1,0:T(8,128)(2,1)S(1)}, bf16[256,128]{1,0:T(8,128)(2,1)S(1)}, u32[]{:S(2)}, u32[]{:S(2)}) collective-permute-start(bf16[256,128]{1,0:T(8,128)(2,1)S(1)} %copy.94), channel_id=1, source_target_pairs={{30,0},{0,2},{2,4},{4,6},{6,8},{8,10},{10,12},{12,14},{14,16},{16,... | collective-permute-start | bytes 196616 | tf_op jit(solution)/shard_map/while/body/eval_jaxpr/ppermute | solution.py:12
  59.8 8.3 %collective-permute-start.1 = (bf16[256,128]{1,0:T(8,128)(2,1)S(1)}, bf16[256,128]{1,0:T(8,128)(2,1)S(1)}, u32[]{:S(2)}, u32[]{:S(2)}) collective-permute-start(bf16[256,128]{1,0:T(8,128)(2,1)S(1)} %copy.94), channel_id=1, source_target_pairs={{30,0},{0,2},{2,4},{4,6},{6,8},{8,10},{10,12},{12,14},{14,16},{16,... | collective-permute-start | bytes 196616 | tf_op jit(solution)/shard_map/while/body/eval_jaxpr/ppermute | solution.py:12
  68.1 7.0 %collective-permute-start.1 = (bf16[256,128]{1,0:T(8,128)(2,1)S(1)}, bf16[256,128]{1,0:T(8,128)(2,1)S(1)}, u32[]{:S(2)}, u32[]{:S(2)}) collective-permute-start(bf16[256,128]{1,0:T(8,128)(2,1)S(1)} %copy.94), channel_id=1, source_target_pairs={{30,0},{0,2},{2,4},{4,6},{6,8},{8,10},{10,12},{12,14},{14,16},{16,... | collective-permute-start | bytes 196616 | tf_op jit(solution)/shard_map/while/body/eval_jaxpr/ppermute | solution.py:12
  75.1 13.4 %copy-start.3 = (bf16[128,128]{1,0:T(8,128)(2,1)S(1)}, bf16[128,128]{1,0:T(8,128)(2,1)}, u32[]{:S(2)}) copy-start(bf16[128,128]{1,0:T(8,128)(2,1)} %param.27) | copy-start | bytes 98308
  75.1 13.4 %copy-start.4 = (bf16[256,128]{1,0:T(8,128)(2,1)S(1)}, bf16[256,128]{1,0:T(8,128)(2,1)}, u32[]{:S(2)}) copy-start(bf16[256,128]{1,0:T(8,128)(2,1)} %param.29) | copy-start | bytes 196612
  75.1 13.4 %copy-start.5 = (f32[128]{0:T(128)S(1)}, f32[128]{0:T(128)}, u32[]{:S(2)}) copy-start(f32[128]{0:T(128)} %param.28) | copy-start | bytes 1540
  75.1 15.1 %copy-start.1 = (bf16[256,128]{1,0:T(8,128)(2,1)S(1)}, bf16[256,128]{1,0:T(8,128)(2,1)}, u32[]{:S(2)}) copy-start(bf16[256,128]{1,0:T(8,128)(2,1)} %param.18) | copy-start | bytes 196612
  75.8 25.8 %copy-start.6 = (s32[1,8]{1,0:T(1,128)S(1)}, s32[1,8]{1,0:T(1,128)}, u32[]{:S(2)}) copy-start(s32[1,8]{1,0:T(1,128)} %get-tuple-element.525) | copy-start | bytes 100
  101.5 231.6 %copy-start.2 = (bf16[128,128]{1,0:T(8,128)(2,1)S(1)}, bf16[128,128]{1,0:T(8,128)(2,1)}, u32[]{:S(2)}) copy-start(bf16[128,128]{1,0:T(8,128)(2,1)} %param.26) | copy-start | bytes 98308
  107.6 4.4 %collective-permute-start = (f32[2,128,128]{2,0,1:T(2,128)S(1)}, f32[2,128,128]{2,0,1:T(2,128)S(1)}, u32[]{:S(2)}, u32[]{:S(2)}) collective-permute-start(f32[2,128,128]{2,0,1:T(2,128)S(1)} %convolution_add_fusion.5), channel_id=1, source_target_pairs={{30,0},{0,2},{2,4},{4,6},{6,8},{8,10},{10,12},{12,14},{14,16},{16,... | collective-permute-start | bytes 393224 | tf_op jit(solution)/shard_map/while/body/eval_jaxpr/ppermute | solution.py:12
  118.1 4.4 %collective-permute-start = (f32[2,128,128]{2,0,1:T(2,128)S(1)}, f32[2,128,128]{2,0,1:T(2,128)S(1)}, u32[]{:S(2)}, u32[]{:S(2)}) collective-permute-start(f32[2,128,128]{2,0,1:T(2,128)S(1)} %convolution_add_fusion.5), channel_id=1, source_target_pairs={{30,0},{0,2},{2,4},{4,6},{6,8},{8,10},{10,12},{12,14},{14,16},{16,... | collective-permute-start | bytes 393224 | tf_op jit(solution)/shard_map/while/body/eval_jaxpr/ppermute | solution.py:12
  128.6 4.4 %collective-permute-start = (f32[2,128,128]{2,0,1:T(2,128)S(1)}, f32[2,128,128]{2,0,1:T(2,128)S(1)}, u32[]{:S(2)}, u32[]{:S(2)}) collective-permute-start(f32[2,128,128]{2,0,1:T(2,128)S(1)} %convolution_add_fusion.5), channel_id=1, source_target_pairs={{30,0},{0,2},{2,4},{4,6},{6,8},{8,10},{10,12},{12,14},{14,16},{16,... | collective-permute-start | bytes 393224 | tf_op jit(solution)/shard_map/while/body/eval_jaxpr/ppermute | solution.py:12
  139.1 5.6 %collective-permute-start = (f32[2,128,128]{2,0,1:T(2,128)S(1)}, f32[2,128,128]{2,0,1:T(2,128)S(1)}, u32[]{:S(2)}, u32[]{:S(2)}) collective-permute-start(f32[2,128,128]{2,0,1:T(2,128)S(1)} %convolution_add_fusion.5), channel_id=1, source_target_pairs={{30,0},{0,2},{2,4},{4,6},{6,8},{8,10},{10,12},{12,14},{14,16},{16,... | collective-permute-start | bytes 393224 | tf_op jit(solution)/shard_map/while/body/eval_jaxpr/ppermute | solution.py:12
  150.7 7.1 %collective-permute-start = (f32[2,128,128]{2,0,1:T(2,128)S(1)}, f32[2,128,128]{2,0,1:T(2,128)S(1)}, u32[]{:S(2)}, u32[]{:S(2)}) collective-permute-start(f32[2,128,128]{2,0,1:T(2,128)S(1)} %convolution_add_fusion.5), channel_id=1, source_target_pairs={{30,0},{0,2},{2,4},{4,6},{6,8},{8,10},{10,12},{12,14},{14,16},{16,... | collective-permute-start | bytes 393224 | tf_op jit(solution)/shard_map/while/body/eval_jaxpr/ppermute | solution.py:12
  163.9 7.1 %collective-permute-start = (f32[2,128,128]{2,0,1:T(2,128)S(1)}, f32[2,128,128]{2,0,1:T(2,128)S(1)}, u32[]{:S(2)}, u32[]{:S(2)}) collective-permute-start(f32[2,128,128]{2,0,1:T(2,128)S(1)} %convolution_add_fusion.5), channel_id=1, source_target_pairs={{30,0},{0,2},{2,4},{4,6},{6,8},{8,10},{10,12},{12,14},{14,16},{16,... | collective-permute-start | bytes 393224 | tf_op jit(solution)/shard_map/while/body/eval_jaxpr/ppermute | solution.py:12
  177.1 7.1 %collective-permute-start = (f32[2,128,128]{2,0,1:T(2,128)S(1)}, f32[2,128,128]{2,0,1:T(2,128)S(1)}, u32[]{:S(2)}, u32[]{:S(2)}) collective-permute-start(f32[2,128,128]{2,0,1:T(2,128)S(1)} %convolution_add_fusion.5), channel_id=1, source_target_pairs={{30,0},{0,2},{2,4},{4,6},{6,8},{8,10},{10,12},{12,14},{14,16},{16,... | collective-permute-start | bytes 393224 | tf_op jit(solution)/shard_map/while/body/eval_jaxpr/ppermute | solution.py:12
  190.3 7.1 %collective-permute-start = (f32[2,128,128]{2,0,1:T(2,128)S(1)}, f32[2,128,128]{2,0,1:T(2,128)S(1)}, u32[]{:S(2)}, u32[]{:S(2)}) collective-permute-start(f32[2,128,128]{2,0,1:T(2,128)S(1)} %convolution_add_fusion.5), channel_id=1, source_target_pairs={{30,0},{0,2},{2,4},{4,6},{6,8},{8,10},{10,12},{12,14},{14,16},{16,... | collective-permute-start | bytes 393224 | tf_op jit(solution)/shard_map/while/body/eval_jaxpr/ppermute | solution.py:12
  197.4 135.7 %collective-permute-start.3 = (f32[2,128,128]{2,0,1:T(2,128)S(1)}, f32[2,128,128]{2,0,1:T(2,128)S(1)}, u32[]{:S(2)}, u32[]{:S(2)}) collective-permute-start(f32[2,128,128]{2,0,1:T(2,128)S(1)} %get-tuple-element.257), channel_id=1, source_target_pairs={{16,0},{18,2},{20,4},{22,6},{24,8},{26,10},{28,12},{30,14},{0,16},... | collective-permute-start | bytes 393224 | tf_op jit(solution)/shard_map/ppermute | solution.py:12
  197.4 135.9 %all-to-all-start.1 = ((f32[16,8,128]{2,1,0:T(8,128)}), f32[16,8,128]{2,1,0:T(8,128)S(1)}, u32[]{:S(2)}, u32[]{:S(2)}) async-start(f32[16,8,128]{2,1,0:T(8,128)} %fusion.46), calls=%async_computation.1 | async-start | bytes 131072 | tf_op jit(solution)/shard_map/all_to_all | solution.py:126
  212.8 118.0 %all-reduce.6.cloned.1.call-start = ((), (), s32[]{:S(2)}) async-start(), calls=%async_computation.2 | async-start | bytes 262144 | tf_op jit(solution)/shard_map/psum | solution.py:100
Sparse Core Ops, SparseCore 0:
  239.3 91.4 all-reduce.5
where the time goes:
time: 356 us; the launch traced here: 352 us
  waiting for transfers between devices  107 us (30%)
  starting transfers between devices  57.6 us (16%)
  blocking collectives  55.5 us (16%)
  matrix products  47.6 us (13%)
  local copies, waits for them, and re-layouts  41.5 us (12%)
  other arithmetic  27.1 us (8%)
  between operations  14.3 us (4%)
    psum x1, waiting for transfers between devices, on_device(): lax.psum((jnp.einsum('nf,nh->fh', features, grad_activation, preferred_el...  91.1 us
    ppermute x17, starting transfers between devices, from_behind(): return lax.ppermute(block, axis, route)  36 us
    psum x1, blocking collectives, on_device(): lax.psum((jnp.einsum('nf,nh->fh', features, grad_activation, preferred_el...  26.3 us
    ppermute x17, waiting for transfers between devices, from_behind(): return lax.ppermute(block, axis, route)  16.3 us
    all_to_all x1, starting transfers between devices, on_device(): lax.all_to_all(back_terms, 'blk', split_axis=0, concat_axis=0, tiled=True)  15.3 us
    dynamic_slice x16, local copies, waits for them, and re-layouts, stop_tiles(): lax.dynamic_index_in_dim(tile_count[0], stop_index, 0, keepdims=False)  15.3 us
    dot_general x8, matrix products, forward_tiles(): jnp.einsum('jab,jbf->jaf', tile_block, picked, preferred_element_type=jnp...  11.6 us
    dot_general x8, matrix products, backward_tiles(): jnp.einsum('jab,jaf->jbf', tile_block, picked, preferred_element_type=jnp...  11.4 us
  transfers between devices with their start and end apart: 20, of which 9 were waited for; matrix products, arithmetic and copies ran while one was open for 18% of the time, Pallas kernels for 0%

commit v1 on v0

v1 whole, which is shorter than its diff:
```python
import functools
import math

import jax
import jax.numpy as jnp
from jax import lax
from jax.experimental import pallas as pl
from jax.experimental.pallas import tpu as pltpu
from jax.sharding import PartitionSpec as P

MESH = pl.DeviceIdType.MESH
F32 = jnp.float32
BF16 = jnp.bfloat16


def mm(a, b, ca=1, cb=0):
    return lax.dot_general(a, b, (((ca,), (cb,)), ((), ())), preferred_element_type=F32)


def remote(src, dst, send, recv, device):
    return pltpu.make_async_remote_copy(
        src_ref=src, dst_ref=dst, send_sem=send, recv_sem=recv, device_id=device, device_id_type=MESH
    )


def kernel(
    blocks, grad_scale,
    features, tile_values, tile_target, tile_source, tile_count, hub_list, hub_count, hub_weight,
    self_weight, neighbor_weight, bias, cotangent,
    output, grad_input, grad_self, grad_neighbor, grad_bias,
    tiles, dense, xsend, xbuf, pick, rows_all, weight_all, total, codes,
    part_send, part_recv, back_send, back_recv, last_send, last_recv,
    aggregate, grad_act, pair_send, pair_recv, src_send, src_recv,
    w_send, w_recv, w_sum, w_out,
    tile_sem, xs, xr, fs, rep_s, rep_r, ps, pr, cs, cr, w1s, w1r, w2s, w2r,
):
    half = tile_values.shape[0]
    slots = tile_values.shape[1]
    tile = tile_values.shape[2]
    rows = features.shape[0]
    width = features.shape[1]
    hubs = hub_list.shape[1]
    chips = blocks // 2
    reach = half // 2
    me = lax.axis_index("blk")
    r = lax.axis_index("rep")
    k = me // 2
    c = me % 2
    partner = {"blk": k * 2 + 1 - c}
    other_rep = {"rep": 1 - r}

    for o in range(half):
        pltpu.make_async_copy(tile_values.at[o], tiles.at[o], tile_sem.at[o]).start()
    barrier = pltpu.get_barrier_semaphore()

    def greet(i, carry):
        pl.semaphore_signal(
            barrier, inc=1, device_id={"blk": (me + i) % blocks}, device_id_type=MESH
        )
        return carry

    lax.fori_loop(1, blocks, greet, 0)
    pl.semaphore_signal(barrier, inc=1, device_id=other_rep, device_id_type=MESH)

    xsend[0:rows, :] = features[...]
    reader = lax.broadcasted_iota(jnp.int32, (blocks, hubs), 0)
    slot = lax.broadcasted_iota(jnp.int32, (blocks, hubs), 1)
    counts = jnp.zeros((blocks, hubs), jnp.int32)
    for i in range(blocks):
        counts = jnp.where(reader == i, hub_count[0, i], counts)
    lists = jnp.where(slot < counts, hub_list[...], -1).astype(F32)
    xsend[rows:, :] = jnp.full((blocks, width), -1.0, BF16)
    xsend[rows:, 0:hubs] = lists.astype(BF16)

    pl.semaphore_wait(barrier, blocks)

    def x_copy(d):
        target = ((k + reach * r + d) % chips) * 2 + c
        return remote(xsend, xbuf.at[2 * d], xs.at[d], xr.at[2 * d], {"blk": target})

    def x_extra():
        target = ((k + reach * r + reach) % chips) * 2
        return remote(xsend, xbuf.at[half - 1], xs.at[reach], xr.at[half - 1], {"blk": target})

    def x_pass(d):
        place = 2 * d + 1 - 2 * c
        return remote(xbuf.at[2 * d], xbuf.at[place], fs.at[d], xr.at[place], partner)

    def x_wait(o):
        pltpu.make_async_copy(xbuf.at[o], xbuf.at[o], xr.at[o]).wait()

    @pl.when(r == 0)
    def _():
        pltpu.make_async_copy(xsend, xbuf.at[0], xr.at[0]).start()

    @pl.when(r == 1)
    def _():
        x_copy(0).start()

    for d in range(1, reach):
        x_copy(d).start()

    @pl.when(c == 1)
    def _():
        x_extra().start()

    def code_body(i, carry):
        o, t = i // slots, i % slots
        live = t < tile_count[0, o]
        codes[i] = jnp.where(live, tile_target[o, t] * 2 + tile_source[o, t], -1)
        return carry

    lax.fori_loop(0, half * slots, code_body, 0)

    step = 32

    def build(o, carry):
        pltpu.make_async_copy(tile_values.at[o], tiles.at[o], tile_sem.at[o]).wait()
        for first in range(0, tile, step):
            sums = [jnp.zeros((step, tile), F32) for _ in range(4)]
            for t in range(slots):
                code = codes[o * slots + t]
                value = tiles[o, t, first : first + step, :].astype(F32)
                for q in range(4):
                    sums[q] = sums[q] + value * (code == q).astype(F32)
            for q in range(4):
                i, j = q // 2, q % 2
                dense[o, i * tile + first : i * tile + first + step, j * tile : (j + 1) * tile] = sums[
                    q
                ].astype(BF16)
        return carry

    for d in range(reach):
        lax.fori_loop(2 * d, 2 * d + 2, build, 0)
        x_wait(2 * d)
        if d == 0:

            @pl.when(c == 0)
            def _():
                x_pass(0).start()

        else:
            x_pass(d).start()

    node = lax.broadcasted_iota(jnp.int32, (rows, width), 0).astype(F32)
    reader_row = lax.broadcasted_iota(jnp.int32, (blocks, width), 0)
    total[...] = jnp.zeros_like(total)

    def forward(o):
        lists = xbuf[o, rows:, :].astype(F32)
        mine = jnp.sum(jnp.where(reader_row == me, lists, 0.0), axis=0, keepdims=True)
        chosen = jnp.where(node == mine, 1.0, 0.0).astype(BF16)
        pick[o] = chosen
        block = xbuf[o, 0:rows, :]
        hub_rows = mm(chosen, block, 0, 0)
        rows_all[o * hubs : (o + 1) * hubs, :] = hub_rows[0:hubs, :].astype(BF16)
        source = (me - half * r - o + 2 * blocks) % blocks
        weight_all[o * hubs : (o + 1) * hubs, :] = hub_weight[source]
        total[...] += mm(dense[o], block)

    for o in range(0, half, 2):
        forward(o)
    for o in range(1, half, 2):
        x_wait(o)
        forward(o)
    part_send[...] = total[...] + mm(weight_all[...], rows_all[...], 0, 0)
    part = remote(part_send, part_recv, rep_s.at[0], rep_r.at[0], other_rep)
    part.start()
    own = mm(features[...], self_weight[...]) + bias[...]
    part.wait()
    aggregate[...] = (part_send[...] + part_recv[...]).astype(BF16)
    pre = own + mm(aggregate[...], neighbor_weight[...])
    gate = 1.0 / (1.0 + jnp.exp(-pre))
    output[...] = (pre * gate).astype(BF16)
    grad_act[...] = (cotangent[...].astype(F32) * gate * (1.0 + pre * (1.0 - gate))).astype(BF16)
    back_send[...] = mm(grad_act[...], neighbor_weight[...], 1, 1)
    back = remote(back_send, back_recv, rep_s.at[1], rep_r.at[1], other_rep)
    back.start()

    chunk = 2 * width // blocks
    padded = w_out.shape[1]
    sums = (mm(features[...], grad_act[...], 0, 0), mm(aggregate[...], grad_act[...], 0, 0))
    column = jnp.sum(grad_act[...].astype(F32), axis=0, keepdims=True)
    column = jnp.broadcast_to(column, (8, column.shape[1]))
    for i in range(blocks):
        which, at = (i * chunk) // width, (i * chunk) % width
        if padded > chunk:
            w_send[i, 0:padded, :] = jnp.zeros((padded, width), F32)
        w_send[i, 0:chunk, :] = sums[which][at : at + chunk, :]
        w_send[i, padded : padded + 8, :] = column
    w_recv[me] = w_send[me]

    def w_first(i):
        peer = (me + i) % blocks
        return remote(w_send.at[peer], w_recv.at[me], w1s.at[i], w1r.at[me], {"blk": peer})

    def w_second(i):
        peer = (me + i) % blocks
        return remote(w_sum, w_out.at[me], w2s.at[i], w2r.at[me], {"blk": peer})

    def run(body, low, high):
        def wrapped(i, carry):
            body(i)
            return carry

        lax.fori_loop(low, high, wrapped, 0)

    run(lambda i: w_first(i).start(), 1, blocks)
    back.wait()
    grad_aggregate = (back_send[...] + back_recv[...]).astype(BF16)
    hub_back = mm(weight_all[...], grad_aggregate).astype(BF16)

    def backward(o):
        return mm(dense[o], grad_aggregate, 0, 0) + mm(
            pick[o][:, 0:hubs], hub_back[o * hubs : (o + 1) * hubs, :]
        )

    def pair_copy(d):
        place = d + 1 - c
        return remote(pair_send.at[d], pair_recv.at[place], ps.at[d], pr.at[place], partner)

    def lone_copy():
        target = ((k - reach * r - reach + 2 * chips) % chips) * 2 + 1
        return remote(
            pair_send.at[reach - 1], src_recv.at[reach], ps.at[reach - 1], cr.at[reach], {"blk": target}
        )

    def pair_wait(d):
        pltpu.make_async_copy(pair_recv.at[d], pair_recv.at[d], pr.at[d]).wait()

    def src_copy(d):
        target = ((k - reach * r - d + 2 * chips) % chips) * 2 + c
        return remote(src_send.at[d], src_recv.at[d], cs.at[d], cr.at[d], {"blk": target})

    def src_wait(d):
        pltpu.make_async_copy(src_recv.at[d], src_recv.at[d], cr.at[d]).wait()

    for d in range(reach - 1, -1, -1):
        pair_send[d] = backward(2 * d + 1).astype(BF16)
        if d == reach - 1:

            @pl.when(c == 0)
            def _():
                lone_copy().start()

            @pl.when(c == 1)
            def _():
                pair_copy(reach - 1).start()

        else:
            pair_copy(d).start()
    for d in range(reach - 1, -1, -1):
        if d > 0:
            term = backward(2 * d)
            pair_wait(d)
            src_send[d] = (term + pair_recv[d].astype(F32)).astype(BF16)
            src_copy(d).start()
        else:
            total[...] = backward(0)

            @pl.when(c == 0)
            def _():
                pair_wait(0)
                total[...] += pair_recv[0].astype(F32)

            src_send[0] = total[...].astype(BF16)

            @pl.when(r == 0)
            def _():
                pltpu.make_async_copy(src_send.at[0], src_recv.at[0], cr.at[0]).start()

            @pl.when(r == 1)
            def _():
                src_copy(0).start()

    def w_wait_first(i):
        peer = (me + i) % blocks
        pltpu.make_async_copy(w_recv.at[peer], w_recv.at[peer], w1r.at[peer]).wait()

    run(w_wait_first, 1, blocks)
    reduced = w_recv[0]
    for i in range(1, blocks):
        reduced = reduced + w_recv[i]
    reduced = reduced * grad_scale
    w_sum[...] = reduced[0:padded, :]
    grad_bias[...] = reduced[padded : padded + 1, :]
    w_out[me] = reduced[0:padded, :]
    run(lambda i: w_second(i).start(), 1, blocks)

    total[...] = mm(grad_act[...], self_weight[...], 1, 1)
    for d in range(reach):
        src_wait(d)
        total[...] += src_recv[d].astype(F32)

    @pl.when(c == 1)
    def _():
        src_wait(reach)
        total[...] += src_recv[reach].astype(F32)

    last_send[...] = total[...]
    last = remote(last_send, last_recv, rep_s.at[2], rep_r.at[2], other_rep)
    last.start()

    def w_wait_second(i):
        peer = (me + i) % blocks
        pltpu.make_async_copy(w_out.at[peer], w_out.at[peer], w2r.at[peer]).wait()

    run(w_wait_second, 1, blocks)
    for i in range(blocks):
        which, at = (i * chunk) // width, (i * chunk) % width
        (grad_self, grad_neighbor)[which][at : at + chunk, :] = w_out[i, 0:chunk, :]
    last.wait()
    grad_input[...] = (last_send[...] + last_recv[...]).astype(BF16)

    @pl.when(r == 1)
    def _():
        x_copy(0).wait_send()
        src_copy(0).wait_send()

    for d in range(1, reach):
        x_copy(d).wait_send()
        x_pass(d).wait_send()
        src_copy(d).wait_send()

    for d in range(reach - 1):
        pair_copy(d).wait_send()

    @pl.when(c == 0)
    def _():
        x_pass(0).wait_send()
        lone_copy().wait_send()

    @pl.when(c == 1)
    def _():
        x_extra().wait_send()
        pair_copy(reach - 1).wait_send()

    run(lambda i: w_first(i).wait_send(), 1, blocks)
    run(lambda i: w_second(i).wait_send(), 1, blocks)


def on_device(
    features, tile_values, tile_target, tile_source, tile_count, hub_list, hub_count, hub_weight,
    self_weight, neighbor_weight, bias, cotangent,
):
    blocks = lax.axis_size("blk")
    rows, width = features.shape
    half, slots, tile = tile_values.shape[1:4]
    hubs = hub_list.shape[-1]
    hidden = self_weight.shape[1]
    reach = half // 2
    chunk = 2 * width // blocks
    padded = max(chunk, 8)
    grad_scale = 1.0 / math.sqrt(rows * blocks)
    vmem = pl.BlockSpec(memory_space=pltpu.VMEM)
    smem = pl.BlockSpec(memory_space=pltpu.SMEM)
    dma = pltpu.SemaphoreType.DMA
    V = pltpu.VMEM
    block = (rows, width)
    scratch = [
        V((half, slots, tile, tile), BF16),
        V((half, rows, rows), BF16),
        V((rows + blocks, width), BF16),
        V((half, rows + blocks, width), BF16),
        V((half, rows, width), BF16),
        V((half * hubs, width), BF16),
        V((half * hubs, rows), BF16),
        V(block, F32),
        pltpu.SMEM((half * slots,), jnp.int32),
        V(block, F32), V(block, F32),
        V(block, F32), V(block, F32),
        V(block, F32), V(block, F32),
        V(block, BF16),
        V((rows, hidden), BF16),
        V((reach,) + block, BF16), V((reach,) + block, BF16),
        V((reach,) + block, BF16), V((reach + 1,) + block, BF16),
        V((blocks, padded + 8, hidden), F32), V((blocks, padded + 8, hidden), F32),
        V((padded, hidden), F32), V((blocks, padded, hidden), F32),
        dma((half,)),
        dma((reach + 1,)), dma((half,)), dma((reach,)),
        dma((3,)), dma((3,)),
        dma((reach,)), dma((reach,)),
        dma((reach,)), dma((reach + 1,)),
        dma((blocks,)), dma((blocks,)), dma((blocks,)), dma((blocks,)),
    ]
    out = pl.pallas_call(
        functools.partial(kernel, blocks, grad_scale),
        out_shape=(
            jax.ShapeDtypeStruct((rows, hidden), BF16),
            jax.ShapeDtypeStruct((rows, width), BF16),
            jax.ShapeDtypeStruct((width, hidden), F32),
            jax.ShapeDtypeStruct((width, hidden), F32),
            jax.ShapeDtypeStruct((1, hidden), F32),
        ),
        in_specs=[
            vmem, pl.BlockSpec(memory_space=pl.ANY), smem, smem, smem, vmem, smem, vmem,
            vmem, vmem, vmem, vmem,
        ],
        out_specs=(vmem,) * 5,
        scratch_shapes=scratch,
        compiler_params=pltpu.CompilerParams(
            collective_id=0, has_side_effects=True, vmem_limit_bytes=56 * 1024 * 1024
        ),
    )(
        features, tile_values[0], tile_target[0], tile_source[0], tile_count, hub_list[0],
        hub_count, hub_weight, self_weight, neighbor_weight, bias.reshape(1, hidden), cotangent,
    )
    return out[0], out[1], out[2], out[3], out[4].reshape(hidden)


def solution(mesh):
    in_specs = (
        P("blk", None),
        P("blk", "rep", None, None, None),
        P("blk", "rep", None),
        P("blk", "rep", None),
        P("blk", "rep"),
        P("blk", None, None),
        P("blk", None),
        P(None, None, "blk"),
        P(None, "rep"),
        P(None, "rep"),
        P("rep"),
        P("blk", "rep"),
    )
    out_specs = (P("blk", "rep"), P("blk", None), P(None, "rep"), P(None, "rep"), P("rep"))
    return jax.shard_map(
        on_device, mesh=mesh, in_specs=in_specs, out_specs=out_specs, check_vma=False
    )
```

time: 356 us -> 53.9 us (0.15); the launches traced: 352 us -> 53.6 us
  waiting for transfers between devices: 107 us -> 0 us
  starting transfers between devices: 57.6 us -> 0 us
  blocking collectives: 55.5 us -> 0 us
  matrix products: 47.6 us -> 0 us
  Pallas kernels: 0 us -> 45.9 us
  local copies, waits for them, and re-layouts: 41.5 us -> 7.02 us
  other arithmetic: 27.1 us -> 0 us
  between operations: 14.3 us -> 0.65 us
    psum x1 -> x0, waiting for transfers between devices: 91.1 us -> none  [on_device(): lax.psum((jnp.einsum('nf,nh->fh', features, grad_activation, preferred_el...]
    psum x4 -> x0, blocking collectives: 55.5 us -> none  [the longest x1 26.3 us: on_device(): lax.psum((jnp.einsum('nf,nh->fh', features, grad_activation, preferred_el...]
    dot_general x40 -> x0, matrix products: 47.6 us -> none  [the longest x8 11.6 us: forward_tiles(): jnp.einsum('jab,jbf->jaf', tile_block, picked, preferred_element_type=jnp...]
    pallas_call x0 -> x1, Pallas kernels: none -> 45.9 us  [on_device(): pl.pallas_call(functools.partial(kernel, blocks, grad_scale), out_shape=(...]
    ppermute x17 -> x0, starting transfers between devices: 36 us -> none  [from_behind(): return lax.ppermute(block, axis, route)]
    all_to_all x2 -> x0, starting transfers between devices: 21.6 us -> none  [the longest x1 15.3 us: on_device(): lax.all_to_all(back_terms, 'blk', split_axis=0, concat_axis=0, tiled=True)]
    ppermute x17 -> x0, waiting for transfers between devices: 16.3 us -> none  [from_behind(): return lax.ppermute(block, axis, route)]
    dynamic_slice x18 -> x0, local copies, waits for them, and re-layouts: 16.1 us -> none  [the longest x16 15.3 us: stop_tiles(): lax.dynamic_index_in_dim(tile_count[0], stop_index, 0, keepdims=False)]
  transfers between devices with their start and end apart: 20 -> 0, of which waited for: 9 -> 0; matrix products, arithmetic and copies ran while one was open for 18% -> 0% of each run, Pallas kernels for 0% -> 0%
where the time goes in v1:
time: 53.9 us; the launch traced here: 53.6 us
  Pallas kernels  45.9 us (85%)
  local copies, waits for them, and re-layouts  7.02 us (13%)
  between operations  0.65 us (1%)
    pallas_call x1, Pallas kernels, on_device(): pl.pallas_call(functools.partial(kernel, blocks, grad_scale), out_shape=(...  45.9 us
    unnamed x5, local copies, waits for them, and re-layouts  7.02 us

profile of v1, /device:TPU:26, one launch (start us, length us, event | category | flops | bytes accessed | tf_op | source)
XLA Modules:
  0.0 53.6 jit_solution(7302574078214408326)
XLA Ops:
  0.6 45.9 %shard_map.155 = (bf16[256,128]{1,0:T(8,128)(2,1)}, bf16[256,128]{1,0:T(8,128)(2,1)}, f32[128,128]{1,0:T(8,128)}, f32[128,128]{1,0:T(8,128)}, f32[1,128]{1,0:T(1,128)}) custom-call(bf16[256,128]{1,0:T(8,128)(2,1)} %features.1, bf16[8,16,128,128]{3,2,1,0:T(8,128)(2,1)} %bitcast.6, s32[8,16]{1,0:T(8,128)} %bitcast.8, s32[8,16]{1,0:T(8,128)} %bitcast.9, ...), custom_call_target="tpu_custom_call" | custom-call | tf_op jit(solution)/shard_map/pallas_call | solution.py:386
  46.6 1.5 %copy.22 = bf16[256,128]{1,0:T(8,128)(2,1)} copy(bf16[256,128]{1,0:T(8,128)(2,1)} %get-tuple-element.20) | data formatting | bytes 131072
  48.0 1.5 %copy.23 = bf16[256,128]{1,0:T(8,128)(2,1)} copy(bf16[256,128]{1,0:T(8,128)(2,1)} %get-tuple-element.21) | data formatting | bytes 131072
  49.5 1.5 %copy.24 = f32[128,128]{1,0:T(8,128)} copy(f32[128,128]{1,0:T(8,128)} %get-tuple-element.22) | data formatting | bytes 131072
  51.0 1.5 %copy.25 = f32[128,128]{1,0:T(8,128)} copy(f32[128,128]{1,0:T(8,128)} %get-tuple-element.23) | data formatting | bytes 131072
  52.5 1.1 %copy.26 = f32[128]{0:T(128)} copy(f32[128]{0:T(128)} %bitcast.11) | data formatting | bytes 1024

commit v2 on v1

--- a/solution.py
+++ b/solution.py
@@ -337,6 +337,11 @@
 
     run(lambda i: w_first(i).wait_send(), 1, blocks)
     run(lambda i: w_second(i).wait_send(), 1, blocks)
+
+
+def finish(*refs):
+    for source, target in zip(refs[:5], refs[5:]):
+        target[...] = source[...]
 
 
 def on_device(
@@ -405,6 +410,12 @@
         features, tile_values[0], tile_target[0], tile_source[0], tile_count, hub_list[0],
         hub_count, hub_weight, self_weight, neighbor_weight, bias.reshape(1, hidden), cotangent,
     )
+    out = pl.pallas_call(
+        finish,
+        out_shape=tuple(jax.ShapeDtypeStruct(x.shape, x.dtype) for x in out),
+        in_specs=[vmem] * 5,
+        out_specs=(vmem,) * 5,
+    )(*out)
     return out[0], out[1], out[2], out[3], out[4].reshape(hidden)
 
 

time: 53.9 us -> 48.4 us (0.90)
  local copies, waits for them, and re-layouts: 7.02 us -> 0 us
  Pallas kernels: 45.9 us -> 47.6 us
    unnamed x5 -> x0, local copies, waits for them, and re-layouts: 7.02 us -> none
    pallas_call x0 -> x1, Pallas kernels: none -> 1.64 us  [on_device(): pl.pallas_call(finish, out_shape=tuple((jax.ShapeDtypeStruct(x.shape, x.d...]
where the time goes in v2:
time: 48.4 us; the launch traced here: 48.2 us
  Pallas kernels  47.6 us (98%)
  between operations  0.64 us (1%)
    pallas_call x1, Pallas kernels, on_device(): pl.pallas_call(functools.partial(kernel, blocks, grad_scale), out_shape=(...  45.9 us
    pallas_call x1, Pallas kernels, on_device(): pl.pallas_call(finish, out_shape=tuple((jax.ShapeDtypeStruct(x.shape, x.d...  1.64 us

profile of v2, /device:TPU:26, one launch (start us, length us, event | category | flops | bytes accessed | tf_op | source)
XLA Modules:
  0.0 48.2 jit_solution(9890147918462423025)
XLA Ops:
  0.6 45.9 %shard_map.155 = (bf16[256,128]{1,0:T(8,128)(2,1)}, bf16[256,128]{1,0:T(8,128)(2,1)}, f32[128,128]{1,0:T(8,128)}, f32[128,128]{1,0:T(8,128)}, f32[1,128]{1,0:T(1,128)}) custom-call(bf16[256,128]{1,0:T(8,128)(2,1)} %features.1, bf16[8,16,128,128]{3,2,1,0:T(8,128)(2,1)} %bitcast.6, s32[8,16]{1,0:T(8,128)} %bitcast.8, s32[8,16]{1,0:T(8,128)} %bitcast.9, ...), custom_call_target="tpu_custom_call" | custom-call | tf_op jit(solution)/shard_map/pallas_call | solution.py:391
  46.6 1.6 %shard_map.156 = (bf16[256,128]{1,0:T(8,128)(2,1)}, bf16[256,128]{1,0:T(8,128)(2,1)}, f32[128,128]{1,0:T(8,128)}, f32[128,128]{1,0:T(8,128)}, f32[1,128]{1,0:T(1,128)}) custom-call(bf16[256,128]{1,0:T(8,128)(2,1)} %get-tuple-element.15.refs_0_, bf16[256,128]{1,0:T(8,128)(2,1)} %get-tuple-element.16.refs_1_, f32[128,128]{1,0:T(8,128)} %get-tuple-element.17.refs_2_, ...), custom_call_target="tpu_custom_call" | custom-call | tf_op jit(solution)/shard_map/pallas_call | solution.py:413

commit v3 on v2

--- a/solution.py
+++ b/solution.py
@@ -28,7 +28,7 @@
     features, tile_values, tile_target, tile_source, tile_count, hub_list, hub_count, hub_weight,
     self_weight, neighbor_weight, bias, cotangent,
     output, grad_input, grad_self, grad_neighbor, grad_bias,
-    tiles, dense, xsend, xbuf, pick, rows_all, weight_all, total, codes,
+    tiles, dense, dense_t, xsend, xbuf, pick, rows_all, weight_all, weight_t, total, codes,
     part_send, part_recv, back_send, back_recv, last_send, last_recv,
     aggregate, grad_act, pair_send, pair_recv, src_send, src_recv,
     w_send, w_recv, w_sum, w_out,
@@ -128,7 +128,13 @@
                 dense[o, i * tile + first : i * tile + first + step, j * tile : (j + 1) * tile] = sums[
                     q
                 ].astype(BF16)
+        dense_t[o] = dense[o].T
         return carry
+
+    for o in range(half):
+        source = (me - half * r - o + 2 * blocks) % blocks
+        weight_all[o * hubs : (o + 1) * hubs, :] = hub_weight[source]
+    weight_t[...] = weight_all[...].T
 
     for d in range(reach):
         lax.fori_loop(2 * d, 2 * d + 2, build, 0)
@@ -143,19 +149,19 @@
             x_pass(d).start()
 
     node = lax.broadcasted_iota(jnp.int32, (rows, width), 0).astype(F32)
+    node_lane = lax.broadcasted_iota(jnp.int32, (hubs, rows), 1).astype(F32)
     reader_row = lax.broadcasted_iota(jnp.int32, (blocks, width), 0)
     total[...] = jnp.zeros_like(total)
 
+    def hub_row(o):
+        lists = xbuf[o, rows:, :].astype(F32)
+        return jnp.sum(jnp.where(reader_row == me, lists, 0.0), axis=0, keepdims=True)
+
     def forward(o):
-        lists = xbuf[o, rows:, :].astype(F32)
-        mine = jnp.sum(jnp.where(reader_row == me, lists, 0.0), axis=0, keepdims=True)
-        chosen = jnp.where(node == mine, 1.0, 0.0).astype(BF16)
-        pick[o] = chosen
+        column = jnp.broadcast_to(hub_row(o), (8, width)).T[0:hubs, 0:1]
+        chosen = jnp.where(node_lane == column, 1.0, 0.0).astype(BF16)
         block = xbuf[o, 0:rows, :]
-        hub_rows = mm(chosen, block, 0, 0)
-        rows_all[o * hubs : (o + 1) * hubs, :] = hub_rows[0:hubs, :].astype(BF16)
-        source = (me - half * r - o + 2 * blocks) % blocks
-        weight_all[o * hubs : (o + 1) * hubs, :] = hub_weight[source]
+        rows_all[o * hubs : (o + 1) * hubs, :] = mm(chosen, block).astype(BF16)
         total[...] += mm(dense[o], block)
 
     for o in range(0, half, 2):
@@ -163,17 +169,21 @@
     for o in range(1, half, 2):
         x_wait(o)
         forward(o)
-    part_send[...] = total[...] + mm(weight_all[...], rows_all[...], 0, 0)
+    total[...] += mm(weight_t[...], rows_all[...])
+    part_send[...] = total[...].astype(BF16)
     part = remote(part_send, part_recv, rep_s.at[0], rep_r.at[0], other_rep)
     part.start()
     own = mm(features[...], self_weight[...]) + bias[...]
+    for o in range(half):
+        pick[o] = jnp.where(node == hub_row(o), 1.0, 0.0).astype(BF16)
     part.wait()
-    aggregate[...] = (part_send[...] + part_recv[...]).astype(BF16)
+    aggregate[...] = (total[...] + part_recv[...].astype(F32)).astype(BF16)
     pre = own + mm(aggregate[...], neighbor_weight[...])
     gate = 1.0 / (1.0 + jnp.exp(-pre))
     output[...] = (pre * gate).astype(BF16)
     grad_act[...] = (cotangent[...].astype(F32) * gate * (1.0 + pre * (1.0 - gate))).astype(BF16)
-    back_send[...] = mm(grad_act[...], neighbor_weight[...], 1, 1)
+    total[...] = mm(grad_act[...], neighbor_weight[...], 1, 1)
+    back_send[...] = total[...].astype(BF16)
     back = remote(back_send, back_recv, rep_s.at[1], rep_r.at[1], other_rep)
     back.start()
 
@@ -205,13 +215,12 @@
 
         lax.fori_loop(low, high, wrapped, 0)
 
-    run(lambda i: w_first(i).start(), 1, blocks)
     back.wait()
-    grad_aggregate = (back_send[...] + back_recv[...]).astype(BF16)
+    grad_aggregate = (total[...] + back_recv[...].astype(F32)).astype(BF16)
     hub_back = mm(weight_all[...], grad_aggregate).astype(BF16)
 
     def backward(o):
-        return mm(dense[o], grad_aggregate, 0, 0) + mm(
+        return mm(dense_t[o], grad_aggregate) + mm(
             pick[o][:, 0:hubs], hub_back[o * hubs : (o + 1) * hubs, :]
         )
 
@@ -249,6 +258,7 @@
 
         else:
             pair_copy(d).start()
+    run(lambda i: w_first(i).start(), 1, blocks)
     for d in range(reach - 1, -1, -1):
         if d > 0:
             term = backward(2 * d)
@@ -297,7 +307,7 @@
         src_wait(reach)
         total[...] += src_recv[reach].astype(F32)
 
-    last_send[...] = total[...]
+    last_send[...] = total[...].astype(BF16)
     last = remote(last_send, last_recv, rep_s.at[2], rep_r.at[2], other_rep)
     last.start()
 
@@ -310,7 +320,7 @@
         which, at = (i * chunk) // width, (i * chunk) % width
         (grad_self, grad_neighbor)[which][at : at + chunk, :] = w_out[i, 0:chunk, :]
     last.wait()
-    grad_input[...] = (last_send[...] + last_recv[...]).astype(BF16)
+    grad_input[...] = (last_send[...].astype(F32) + last_recv[...].astype(F32)).astype(BF16)
 
     @pl.when(r == 1)
     def _():
@@ -365,16 +375,18 @@
     scratch = [
         V((half, slots, tile, tile), BF16),
         V((half, rows, rows), BF16),
+        V((half, rows, rows), BF16),
         V((rows + blocks, width), BF16),
         V((half, rows + blocks, width), BF16),
         V((half, rows, width), BF16),
         V((half * hubs, width), BF16),
         V((half * hubs, rows), BF16),
+        V((rows, half * hubs), BF16),
         V(block, F32),
         pltpu.SMEM((half * slots,), jnp.int32),
-        V(block, F32), V(block, F32),
-        V(block, F32), V(block, F32),
-        V(block, F32), V(block, F32),
+        V(block, BF16), V(block, BF16),
+        V(block, BF16), V(block, BF16),
+        V(block, BF16), V(block, BF16),
         V(block, BF16),
         V((rows, hidden), BF16),
         V((reach,) + block, BF16), V((reach,) + block, BF16),

time: 48.4 us -> 47.8 us (0.988)
  Pallas kernels: 47.6 us -> 46.9 us
    pallas_call x1, Pallas kernels: 45.9 us -> 45.3 us  [on_device(): pl.pallas_call(functools.partial(kernel, blocks, grad_scale), out_shape=(...]
where the time goes in v3:
time: 47.8 us; the launch traced here: 47.6 us
  Pallas kernels  46.9 us (98%)
  between operations  0.64 us (1%)
    pallas_call x1, Pallas kernels, on_device(): pl.pallas_call(functools.partial(kernel, blocks, grad_scale), out_shape=(...  45.3 us
    pallas_call x1, Pallas kernels, on_device(): pl.pallas_call(finish, out_shape=tuple((jax.ShapeDtypeStruct(x.shape, x.d...  1.64 us

profile of v3, /device:TPU:26, one launch (start us, length us, event | category | flops | bytes accessed | tf_op | source)
XLA Modules:
  0.0 47.6 jit_solution(13249441199796935888)
XLA Ops:
  0.6 45.3 %shard_map.155 = (bf16[256,128]{1,0:T(8,128)(2,1)}, bf16[256,128]{1,0:T(8,128)(2,1)}, f32[128,128]{1,0:T(8,128)}, f32[128,128]{1,0:T(8,128)}, f32[1,128]{1,0:T(1,128)}) custom-call(bf16[256,128]{1,0:T(8,128)(2,1)} %features.1, bf16[8,16,128,128]{3,2,1,0:T(8,128)(2,1)} %bitcast.6, s32[8,16]{1,0:T(8,128)} %bitcast.8, s32[8,16]{1,0:T(8,128)} %bitcast.9, ...), custom_call_target="tpu_custom_call" | custom-call | tf_op jit(solution)/shard_map/pallas_call | solution.py:403
  45.9 1.6 %shard_map.156 = (bf16[256,128]{1,0:T(8,128)(2,1)}, bf16[256,128]{1,0:T(8,128)(2,1)}, f32[128,128]{1,0:T(8,128)}, f32[128,128]{1,0:T(8,128)}, f32[1,128]{1,0:T(1,128)}) custom-call(bf16[256,128]{1,0:T(8,128)(2,1)} %get-tuple-element.15.refs_0_, bf16[256,128]{1,0:T(8,128)(2,1)} %get-tuple-element.16.refs_1_, f32[128,128]{1,0:T(8,128)} %get-tuple-element.17.refs_2_, ...), custom_call_target="tpu_custom_call" | custom-call | tf_op jit(solution)/shard_map/pallas_call | solution.py:425

commit v4 on v3

--- a/solution.py
+++ b/solution.py
@@ -32,7 +32,7 @@
     part_send, part_recv, back_send, back_recv, last_send, last_recv,
     aggregate, grad_act, pair_send, pair_recv, src_send, src_recv,
     w_send, w_recv, w_sum, w_out,
-    tile_sem, xs, xr, fs, rep_s, rep_r, ps, pr, cs, cr, w1s, w1r, w2s, w2r,
+    tile_sem, xs, xr, fs, rl, rep_s, rep_r, ps, pr, cs, cr, w1s, w1r, w2s, w2r,
 ):
     half = tile_values.shape[0]
     slots = tile_values.shape[1]
@@ -86,6 +86,14 @@
         place = 2 * d + 1 - 2 * c
         return remote(xbuf.at[2 * d], xbuf.at[place], fs.at[d], xr.at[place], partner)
 
+    def x_direct(d):
+        return (k + reach * r + d) % 2 == 0
+
+    def x_relay(d):
+        return remote(
+            xbuf.at[2 * d], xbuf.at[2 * d + 2], rl.at[d], xr.at[2 * d + 2], {"blk": (me + 2) % blocks}
+        )
+
     def x_wait(o):
         pltpu.make_async_copy(xbuf.at[o], xbuf.at[o], xr.at[o]).wait()
 
@@ -98,7 +106,10 @@
         x_copy(0).start()
 
     for d in range(1, reach):
-        x_copy(d).start()
+
+        @pl.when(x_direct(d))
+        def _():
+            x_copy(d).start()
 
     @pl.when(c == 1)
     def _():
@@ -139,6 +150,12 @@
     for d in range(reach):
         lax.fori_loop(2 * d, 2 * d + 2, build, 0)
         x_wait(2 * d)
+        if d < reach - 1:
+
+            @pl.when(k % 2 == 0)
+            def _():
+                x_relay(d).start()
+
         if d == 0:
 
             @pl.when(c == 0)
@@ -258,7 +275,6 @@
 
         else:
             pair_copy(d).start()
-    run(lambda i: w_first(i).start(), 1, blocks)
     for d in range(reach - 1, -1, -1):
         if d > 0:
             term = backward(2 * d)
@@ -282,6 +298,8 @@
             @pl.when(r == 1)
             def _():
                 src_copy(0).start()
+
+    run(lambda i: w_first(i).start(), 1, blocks)
 
     def w_wait_first(i):
         peer = (me + i) % blocks
@@ -307,7 +325,7 @@
         src_wait(reach)
         total[...] += src_recv[reach].astype(F32)
 
-    last_send[...] = total[...].astype(BF16)
+    last_send[...] = total[...]
     last = remote(last_send, last_recv, rep_s.at[2], rep_r.at[2], other_rep)
     last.start()
 
@@ -320,7 +338,7 @@
         which, at = (i * chunk) // width, (i * chunk) % width
         (grad_self, grad_neighbor)[which][at : at + chunk, :] = w_out[i, 0:chunk, :]
     last.wait()
-    grad_input[...] = (last_send[...].astype(F32) + last_recv[...].astype(F32)).astype(BF16)
+    grad_input[...] = (last_send[...] + last_recv[...]).astype(BF16)
 
     @pl.when(r == 1)
     def _():
@@ -328,7 +346,15 @@
         src_copy(0).wait_send()
 
     for d in range(1, reach):
-        x_copy(d).wait_send()
+
+        @pl.when(x_direct(d))
+        def _():
+            x_copy(d).wait_send()
+
+        @pl.when(k % 2 == 0)
+        def _():
+            x_relay(d - 1).wait_send()
+
         x_pass(d).wait_send()
         src_copy(d).wait_send()
 
@@ -386,7 +412,7 @@
         pltpu.SMEM((half * slots,), jnp.int32),
         V(block, BF16), V(block, BF16),
         V(block, BF16), V(block, BF16),
-        V(block, BF16), V(block, BF16),
+        V(block, F32), V(block, F32),
         V(block, BF16),
         V((rows, hidden), BF16),
         V((reach,) + block, BF16), V((reach,) + block, BF16),
@@ -394,7 +420,7 @@
         V((blocks, padded + 8, hidden), F32), V((blocks, padded + 8, hidden), F32),
         V((padded, hidden), F32), V((blocks, padded, hidden), F32),
         dma((half,)),
-        dma((reach + 1,)), dma((half,)), dma((reach,)),
+        dma((reach + 1,)), dma((half,)), dma((reach,)), dma((reach,)),
         dma((3,)), dma((3,)),
         dma((reach,)), dma((reach,)),
         dma((reach,)), dma((reach + 1,)),

time: 47.8 us -> 52.4 us (1.096)
  the two profiles are of different devices: /device:TPU:26 before, /device:TPU:0 now
where the time goes in v4:
time: 52.4 us; the launch traced here: 52.2 us
  Pallas kernels  51.5 us (98%)
  between operations  0.64 us (1%)
    pallas_call x1, Pallas kernels, on_device(): pl.pallas_call(functools.partial(kernel, blocks, grad_scale), out_shape=(...  49.9 us
    pallas_call x1, Pallas kernels, on_device(): pl.pallas_call(finish, out_shape=tuple((jax.ShapeDtypeStruct(x.shape, x.d...  1.64 us

profile of v4, /device:TPU:0, one launch (start us, length us, event | category | flops | bytes accessed | tf_op | source)
XLA Modules:
  0.0 52.2 jit_solution(5254239426839683803)
XLA Ops:
  0.6 49.9 %shard_map.155 = (bf16[256,128]{1,0:T(8,128)(2,1)}, bf16[256,128]{1,0:T(8,128)(2,1)}, f32[128,128]{1,0:T(8,128)}, f32[128,128]{1,0:T(8,128)}, f32[1,128]{1,0:T(1,128)}) custom-call(bf16[256,128]{1,0:T(8,128)(2,1)} %features.1, bf16[8,16,128,128]{3,2,1,0:T(8,128)(2,1)} %bitcast.6, s32[8,16]{1,0:T(8,128)} %bitcast.8, s32[8,16]{1,0:T(8,128)} %bitcast.9, ...), custom_call_target="tpu_custom_call" | custom-call | tf_op jit(solution)/shard_map/pallas_call | solution.py:429
  50.5 1.6 %shard_map.156 = (bf16[256,128]{1,0:T(8,128)(2,1)}, bf16[256,128]{1,0:T(8,128)(2,1)}, f32[128,128]{1,0:T(8,128)}, f32[128,128]{1,0:T(8,128)}, f32[1,128]{1,0:T(1,128)}) custom-call(bf16[256,128]{1,0:T(8,128)(2,1)} %get-tuple-element.15.refs_0_, bf16[256,128]{1,0:T(8,128)(2,1)} %get-tuple-element.16.refs_1_, f32[128,128]{1,0:T(8,128)} %get-tuple-element.17.refs_2_, ...), custom_call_target="tpu_custom_call" | custom-call | tf_op jit(solution)/shard_map/pallas_call | solution.py:451

commit v5 on v3

--- a/solution.py
+++ b/solution.py
@@ -215,6 +215,7 @@
 
         lax.fori_loop(low, high, wrapped, 0)
 
+    run(lambda i: w_first(i).start(), 1, blocks)
     back.wait()
     grad_aggregate = (total[...] + back_recv[...].astype(F32)).astype(BF16)
     hub_back = mm(weight_all[...], grad_aggregate).astype(BF16)
@@ -258,7 +259,6 @@
 
         else:
             pair_copy(d).start()
-    run(lambda i: w_first(i).start(), 1, blocks)
     for d in range(reach - 1, -1, -1):
         if d > 0:
             term = backward(2 * d)

time: 47.8 us -> 45.1 us (0.944)
  Pallas kernels: 46.9 us -> 44.3 us
    pallas_call x1, Pallas kernels: 45.3 us -> 42.7 us  [on_device(): pl.pallas_call(functools.partial(kernel, blocks, grad_scale), out_shape=(...]
where the time goes in v5:
time: 45.1 us; the launch traced here: 45 us
  Pallas kernels  44.3 us (98%)
  between operations  0.64 us (1%)
    pallas_call x1, Pallas kernels, on_device(): pl.pallas_call(functools.partial(kernel, blocks, grad_scale), out_shape=(...  42.7 us
    pallas_call x1, Pallas kernels, on_device(): pl.pallas_call(finish, out_shape=tuple((jax.ShapeDtypeStruct(x.shape, x.d...  1.64 us

profile of v5, /device:TPU:26, one launch (start us, length us, event | category | flops | bytes accessed | tf_op | source)
XLA Modules:
  0.0 45.0 jit_solution(17734931761550314956)
XLA Ops:
  0.6 42.7 %shard_map.155 = (bf16[256,128]{1,0:T(8,128)(2,1)}, bf16[256,128]{1,0:T(8,128)(2,1)}, f32[128,128]{1,0:T(8,128)}, f32[128,128]{1,0:T(8,128)}, f32[1,128]{1,0:T(1,128)}) custom-call(bf16[256,128]{1,0:T(8,128)(2,1)} %features.1, bf16[8,16,128,128]{3,2,1,0:T(8,128)(2,1)} %bitcast.6, s32[8,16]{1,0:T(8,128)} %bitcast.8, s32[8,16]{1,0:T(8,128)} %bitcast.9, ...), custom_call_target="tpu_custom_call" | custom-call | tf_op jit(solution)/shard_map/pallas_call | solution.py:403
  43.3 1.6 %shard_map.156 = (bf16[256,128]{1,0:T(8,128)(2,1)}, bf16[256,128]{1,0:T(8,128)(2,1)}, f32[128,128]{1,0:T(8,128)}, f32[128,128]{1,0:T(8,128)}, f32[1,128]{1,0:T(1,128)}) custom-call(bf16[256,128]{1,0:T(8,128)(2,1)} %get-tuple-element.15.refs_0_, bf16[256,128]{1,0:T(8,128)(2,1)} %get-tuple-element.16.refs_1_, f32[128,128]{1,0:T(8,128)} %get-tuple-element.17.refs_2_, ...), custom_call_target="tpu_custom_call" | custom-call | tf_op jit(solution)/shard_map/pallas_call | solution.py:425
